TPU v7x, 32 devices: a whole 2x2x4 slice. The times are simulated.
32 devices in a mesh: row: 8 (over y, x, core), col: 4 (over z).
Axes of the slice: x: 2, y: 2, z: 4, core: 2. Of those that a mesh axis runs over, the one named last changes fastest.
Arguments:
- tiles: bfloat16 [8, 4, 80, 256, 256], P('row', 'col'), may hold values from -0.125 to 0.125
- tile_coords: int32 [2, 8, 4, 80], P(None, 'row', 'col'), may hold values from 0 to 1023, as said below
- tile_counts: int32 [8, 4], P('row', 'col'), may hold values from 40 to 80, as said below
- vectors: bfloat16 [262144, 16], P(('row', 'col')), may hold values from -6 to 6
Outputs:
- product: float32 [262144, 16], P(('row', 'col'))
Inputs may be any that keep to these rules, and one draw needn't show every extreme that they name: `tile_coords`: for slot s below tile_counts[r, c]: the tile row I lies in r * 128 to (r + 1) * 128 - 1; the tile column J has (J // 32) % 4 equal to c; when I != J, I < J exactly when I + J is even; no (row, column) pair appears in two live slots anywhere. Among the live slots of one device at most 35 have tile rows in any one run of 32 tile rows, and at most 28 have tile columns in any one run of 32 tile columns; a device with all slots live reaches both. Slots at or above the count hold 0. `tile_counts`: some device holds exactly 80 live slots.
All inputs are finite; a program needn't handle non-finite values.
Results may differ from a plain program's by a relative error of at most 0.0075.
Values may be sent and summed in bfloat16 or wider, within the bound.
A program may use at most 320 MiB of HBM per device.

v0:
```python
import jax
import jax.numpy as jnp
from jax import lax
from jax.sharding import PartitionSpec as P


def split_tile(stored, tile_rows, tile_cols):
    size_tile = stored.shape[-1]
    down_idx = jnp.arange(size_tile, dtype=jnp.int32)[:, None]
    across_idx = jnp.arange(size_tile, dtype=jnp.int32)[None, :]
    off_diag = (tile_rows != tile_cols)[:, None, None]
    zero_val = jnp.zeros((), stored.dtype)
    upper_part = jnp.where(off_diag | (down_idx <= across_idx)[None], stored, zero_val)
    lower_part = jnp.where(off_diag | (down_idx < across_idx)[None], stored, zero_val)
    return (upper_part, lower_part)


def shards(tiles, tile_coords, tile_counts, vectors):
    size_tile = tiles.shape[-1]
    slot_count = tiles.shape[2]
    vector_width = vectors.shape[1]
    per_slab = vectors.shape[0] // size_tile
    cols_count = lax.axis_size("col")
    row_here = lax.axis_index("row")
    col_here = lax.axis_index("col")
    stored = tiles.reshape(slot_count, size_tile, size_tile)
    tile_rows = tile_coords[0].reshape(slot_count)
    tile_cols = tile_coords[1].reshape(slot_count)
    live_slots = jnp.arange(slot_count, dtype=jnp.int32) < tile_counts.reshape(())
    row_block = lax.all_gather(vectors, "col", axis=0, tiled=True).reshape(
        -1, size_tile, vector_width
    )
    col_group = lax.all_gather(vectors, "row", axis=0, tiled=True).reshape(
        -1, size_tile, vector_width
    )
    row_local = jnp.where(live_slots, tile_rows - row_here * cols_count * per_slab, 0)
    col_local = tile_cols // per_slab // cols_count * per_slab + tile_cols % per_slab
    col_local = jnp.where(live_slots, col_local, 0)
    upper_part, lower_part = split_tile(stored, tile_rows, tile_cols)
    apply_operator = jnp.einsum(
        "tab,tbv->tav", upper_part, col_group[col_local], preferred_element_type=jnp.float32
    ).astype(jnp.bfloat16)
    mirror = jnp.einsum(
        "tba,tbv->tav", lower_part, row_block[row_local], preferred_element_type=jnp.float32
    ).astype(jnp.bfloat16)
    zero_val = jnp.zeros((), jnp.bfloat16)
    apply_operator = jnp.where(live_slots[:, None, None], apply_operator, zero_val).reshape(
        slot_count, size_tile * vector_width
    )
    mirror = jnp.where(live_slots[:, None, None], mirror, zero_val).reshape(
        slot_count, size_tile * vector_width
    )
    local_row_range = per_slab * size_tile
    panel_start = (row_here * cols_count + col_here) * per_slab
    row_targets = jnp.where(live_slots, tile_rows, -1)
    col_targets = jnp.where(live_slots, tile_cols, -1)

    def merge_into_panel(pieces_in):
        products, destination_rows = pieces_in
        wanted = panel_start + jnp.arange(per_slab, dtype=jnp.int32)
        onehot = (destination_rows[:, None] == wanted[None, :]).astype(jnp.bfloat16)
        return jnp.einsum("ts,tk->sk", onehot, products, preferred_element_type=jnp.float32)

    owned_direct = merge_into_panel(
        (
            lax.all_gather(apply_operator, "col", axis=0, tiled=True),
            lax.all_gather(row_targets, "col", axis=0, tiled=True),
        )
    )
    owned_reflected = merge_into_panel(
        (
            lax.all_gather(mirror, "row", axis=0, tiled=True),
            lax.all_gather(col_targets, "row", axis=0, tiled=True),
        )
    )
    owned_direct = owned_direct.reshape(local_row_range, vector_width)
    owned_reflected = owned_reflected.reshape(local_row_range, vector_width)
    return owned_direct + owned_reflected


def solution(mesh):
    in_specs = (
        P("row", "col", None, None, None),
        P(None, "row", "col", None),
        P("row", "col"),
        P(("row", "col"), None),
    )
    out_specs = P(("row", "col"), None)
    return jax.shard_map(shards, mesh=mesh, in_specs=in_specs, out_specs=out_specs, check_vma=False)
```

profile of v0, /device:TPU:0, one launch (start us, length us, event | category | flops | bytes accessed | tf_op | source)
XLA Modules:
  0.0 183.4 jit_solution(3489110521087887098)
XLA Ops:
  6.5 0.0 all-gather.5.cloned.1.call-start
  6.5 0.7 all-gather.5.cloned.1.call-update
  7.3 0.0 all-gather.9.cloned.1.call-start
  7.3 0.7 all-gather.9.cloned.1.call-update
  8.0 0.0 all-gather.7.cloned.1.call-start
  8.7 0.7 fusion.23
  9.4 0.7 bitcast_compare_fusion
  10.1 29.8 %all-gather.5.cloned.1.call-done = bf16[65536,16]{0,1:T(8,128)(2,1)} async-done(((bf16[8192,16]{0,1:T(8,128)(2,1)}), bf16[65536,16]{0,1:T(8,128)(2,1)}) %all-gather.5.cloned.1.call-update) | async-done | bytes 2097168 | tf_op jit(solution)/shard_map/all_gather | solution.py:33
  39.9 1.7 copy.25
  41.6 0.6 gather_fusion
  42.3 6.9 %fusion.12 = bf16[80,256,16]{1,2,0:T(8,128)(2,1)S(1)} fusion(bf16[80,256,16]{1,2,0:T(8,128)(2,1)S(1)} %gather_fusion, bf16[1,1,80,256,256]{4,3,2,1,0:T(8,128)(2,1)} %param.4, pred[256,256]{1,0:T(8,128)(4,1)S(1)} %iota_compare_fusion.1, pred[80]{0:T(512)(128)(4,1)S(1)} %get-tuple-element.9, pred[80]{0:T(512)(128)(4,1)S(1)} %get-tuple-element.10), kind=kOutput, calls=%fused_computation.18 | convolution fusion | flops 178913280 | bytes 11862176 | tf_op jit(solution)/shard_map/tab,tbv->tav/dot_general | solution.py:40
  49.2 1.3 copy.15
  50.5 1.3 copy.16
  51.8 0.0 all-gather.7.cloned.1.call-update
  51.8 0.0 all-gather.11.cloned.1.call-start
  51.9 17.5 %all-gather.9.cloned.1.call-done = bf16[32768,16]{0,1:T(8,128)(2,1)} async-done(((bf16[8192,16]{0,1:T(8,128)(2,1)}), bf16[32768,16]{0,1:T(8,128)(2,1)}) %all-gather.9.cloned.1.call-update) | async-done | bytes 1048592 | tf_op jit(solution)/shard_map/all_gather | solution.py:30
  69.4 1.3 copy.26
  70.7 0.6 gather_fusion.1
  71.3 0.0 copy-start.2
  71.4 0.0 copy-start.1
  71.4 0.0 copy-start
  71.4 5.6 %fusion.13 = bf16[80,256,16]{1,2,0:T(8,128)(2,1)S(1)} fusion(bf16[80,256,16]{1,2,0:T(8,128)(2,1)S(1)} %gather_fusion.1, bf16[1,1,80,256,256]{4,3,2,1,0:T(8,128)(2,1)} %param.4, pred[256,256]{1,0:T(8,128)(4,1)S(1)} %iota_compare_fusion, pred[80]{0:T(512)(128)(4,1)S(1)} %get-tuple-element.9, pred[80]{0:T(512)(128)(4,1)S(1)} %get-tuple-element.10), kind=kOutput, calls=%fused_computation.19 | convolution fusion | flops 178913280 | bytes 11862176 | tf_op jit(solution)/shard_map/tba,tbv->tav/dot_general | solution.py:43
  77.0 1.3 copy.18
  78.3 1.2 copy.19
  79.5 0.0 all-gather.11.cloned.1.call-update
  79.6 0.0 copy-done.2
  79.6 0.7 dynamic-slice
  80.2 0.0 copy-done.1
  80.2 0.6 dynamic-slice.1
  82.3 0.0 copy-done
  82.3 0.1 fusion.24
  82.4 7.9 %all-reduce = s32[320]{0:T(512)S(1)} all-reduce(s32[320]{0:T(512)S(1)} %get-tuple-element.6), channel_id=1, replica_groups=mesh['row'=8,'col'=4] {'col'}, use_global_device_ids=true, to_apply=%add | all-reduce | flops 320 | bytes 2560
  90.3 8.0 %all-reduce.1 = s32[640]{0:T(1024)S(1)} all-reduce(s32[640]{0:T(1024)S(1)} %get-tuple-element.5), channel_id=1, replica_groups=mesh['row'=8,'col'=4] {'row'}, use_global_device_ids=true, to_apply=%add.1 | all-reduce | flops 640 | bytes 5120
  98.3 27.2 %all-gather.7.cloned.1.call-done = bf16[320,4096]{1,0:T(8,128)(2,1)} async-done(((bf16[80,4096]{1,0:T(8,128)(2,1)}), bf16[320,4096]{1,0:T(8,128)(2,1)}) %all-gather.7.cloned.1.call-update) | async-done | bytes 2621456 | tf_op jit(solution)/shard_map/all_gather | solution.py:66
  125.5 2.4 %fusion.17 = f32[32,4096]{1,0:T(8,128)S(1)} fusion(bf16[320,4096]{1,0:T(8,128)(2,1)} %all-gather.7.cloned.1.call-done, s32[32]{0:T(128)S(1)} %iota_add_fusion, s32[320]{0:T(512)S(1)} %all-reduce), kind=kOutput, calls=%fused_computation.26 | convolution fusion | flops 83896320 | bytes 3147136 | tf_op jit(solution)/shard_map/ts,tk->sk/dot_general | solution.py:62
  127.9 39.2 %all-gather.11.cloned.1.call-done = bf16[640,4096]{1,0:T(8,128)(2,1)} async-done(((bf16[80,4096]{1,0:T(8,128)(2,1)}), bf16[640,4096]{1,0:T(8,128)(2,1)}) %all-gather.11.cloned.1.call-update) | async-done | bytes 5242896 | tf_op jit(solution)/shard_map/all_gather | solution.py:72
  167.1 3.5 %convolution_add_fusion = f32[32,4096]{1,0:T(8,128)S(1)} fusion(f32[32,4096]{1,0:T(8,128)S(1)} %fusion.17, bf16[640,4096]{1,0:T(8,128)(2,1)} %all-gather.11.cloned.1.call-done, s32[32]{0:T(128)S(1)} %iota_add_fusion, s32[640]{0:T(1024)S(1)} %all-reduce.1), kind=kOutput, calls=%fused_computation.14 | convolution fusion | flops 167923712 | bytes 6294144 | tf_op jit(solution)/shard_map/ts,tk->sk/dot_general | solution.py:62
  170.6 2.8 %add.96 = f32[8192,16]{1,0:T(8,128)} reshape(f32[32,4096]{1,0:T(8,128)S(1)} %convolution_add_fusion) | data formatting | bytes 1048576 | tf_op jit(solution)/shard_map/add | solution.py:78
  173.4 3.5 %copy.20 = f32[8192,16]{0,1:T(8,128)} copy(f32[8192,16]{1,0:T(8,128)} %add.96) | data formatting | bytes 1048576 | tf_op jit(solution)/shard_map/add | solution.py:78
  (7 shorter events, 0.1 us)
Async XLA Ops:
  6.5 33.4 %all-gather.5.cloned.1.call-start = ((), (), s32[]{:S(2)}) async-start(), calls=%async_computation | async-start | bytes 2359296 | tf_op jit(solution)/shard_map/all_gather | solution.py:33
  7.3 62.2 %all-gather.9.cloned.1.call-start = ((), (), s32[]{:S(2)}) async-start(), calls=%async_computation.2 | async-start | bytes 1310720 | tf_op jit(solution)/shard_map/all_gather | solution.py:30
  8.0 117.5 %all-gather.7.cloned.1.call-start = ((), (), s32[]{:S(2)}) async-start(), calls=%async_computation.1 | async-start | bytes 3276800 | tf_op jit(solution)/shard_map/all_gather | solution.py:66
  51.8 115.3 %all-gather.11.cloned.1.call-start = ((), (), s32[]{:S(2)}) async-start(), calls=%async_computation.3 | async-start | bytes 5898240 | tf_op jit(solution)/shard_map/all_gather | solution.py:72
  71.3 8.2 %copy-start.2 = (u32[32]{0:T(128)S(1)}, u32[32]{0:T(128)}, u32[]{:S(2)}) copy-start(u32[32]{0:T(128)} %constant.65) | copy-start | bytes 388
  71.4 8.9 %copy-start.1 = (u32[32]{0:T(128)S(1)}, u32[32]{0:T(128)}, u32[]{:S(2)}) copy-start(u32[32]{0:T(128)} %constant.70) | copy-start | bytes 388
  71.4 10.9 %copy-start = (s32[2,1,1,80]{3,2,1,0:T(1,128)S(1)}, s32[2,1,1,80]{3,2,1,0:T(1,128)}, u32[]{:S(2)}) copy-start(s32[2,1,1,80]{3,2,1,0:T(1,128)} %param.5) | copy-start | bytes 1924
Sparse Core Ops, SparseCore 0:
  9.3 30.5 all-gather.4
  41.5 27.9 all-gather.8
  71.0 54.4 all-gather.6
  127.2 39.8 all-gather.10
where the time goes:
time: 184 us; the launch traced here: 183 us
  waiting for transfers between devices  115 us (62%)
  matrix products  18.5 us (10%)
  local copies, waits for them, and re-layouts  17 us (9%)
  blocking collectives  15.9 us (9%)
  between operations  15.3 us (8%)
    all_gather x1, waiting for transfers between devices, shards(): lax.all_gather(mirror, 'row', axis=0, tiled=True)  39.2 us
    all_gather x1, waiting for transfers between devices, shards(): lax.all_gather(vectors, 'row', axis=0, tiled=True)  29.8 us
    all_gather x1, waiting for transfers between devices, shards(): lax.all_gather(apply_operator, 'col', axis=0, tiled=True)  27.2 us
    all_gather x1, waiting for transfers between devices, shards(): lax.all_gather(vectors, 'col', axis=0, tiled=True)  17.5 us
    unnamed x2, blocking collectives  15.9 us
    dot_general x1, matrix products, shards(): jnp.einsum('tab,tbv->tav', upper_part, col_group[col_local], preferred_el...  6.91 us
    add x2, local copies, waits for them, and re-layouts, shards(): return owned_direct + owned_reflected  6.27 us
    dot_general x2, matrix products, merge_into_panel(): jnp.einsum('ts,tk->sk', onehot, products, preferred_element_type=jnp.floa...  5.94 us
  transfers between devices with their start and end apart: 4, of which 4 were waited for; matrix products, arithmetic and copies ran while one was open for 15% of the time, Pallas kernels for 0%

commit v1 on v0

v1 whole, which is shorter than its diff:
```python
import functools

import jax
import jax.numpy as jnp
from jax import lax
from jax.experimental import pallas as pl
from jax.experimental.pallas import tpu as pltpu
from jax.sharding import PartitionSpec as P

MESH = pl.DeviceIdType.MESH
VMEM_LIMIT = 48 * 1024 * 1024
GROUP = 8


def gather_kernel(
    x_ref, xr_ref, xc_ref, own_sem, zs, zr, cs, cr, ss, sr, fs, fr
):
    r, c = lax.axis_index("row"), lax.axis_index("col")
    chip, core = r // 2, r % 2
    sib = 2 * chip + 1 - core

    barrier = pltpu.get_barrier_semaphore()
    for d in range(1, 4):
        pl.semaphore_signal(barrier, inc=1, device_id=(r, (c + d) % 4), device_id_type=MESH)
        pl.semaphore_signal(
            barrier, inc=1, device_id=(2 * ((chip + d) % 4) + core, c), device_id_type=MESH
        )
    pl.semaphore_signal(barrier, inc=1, device_id=(sib, c), device_id_type=MESH)
    pl.semaphore_wait(barrier, 7)

    def z_copy(d, slot):
        return pltpu.make_async_remote_copy(
            x_ref, xr_ref.at[slot], zs.at[d], zr.at[d],
            device_id=(r, (c + d) % 4), device_id_type=MESH,
        )

    def chip_copy(d, slot):
        return pltpu.make_async_remote_copy(
            x_ref, xc_ref.at[slot], cs.at[d], cr.at[d],
            device_id=(2 * ((chip + d) % 4) + core, c), device_id_type=MESH,
        )

    def sib_copy(slot):
        return pltpu.make_async_remote_copy(
            x_ref, xc_ref.at[slot], ss, sr, device_id=(sib, c), device_id_type=MESH
        )

    def fwd_copy(d, slot):
        return pltpu.make_async_remote_copy(
            xc_ref.at[slot], xc_ref.at[slot], fs.at[d], fr.at[d],
            device_id=(sib, c), device_id_type=MESH,
        )

    for d in (2, 1, 3):
        z_copy(d, c).start()
        chip_copy(d, r).start()
    sib_copy(r).start()
    own_r = pltpu.make_async_copy(x_ref, xr_ref.at[c], own_sem.at[0])
    own_c = pltpu.make_async_copy(x_ref, xc_ref.at[r], own_sem.at[1])
    own_r.start()
    own_c.start()
    for d in (2, 1, 3):
        slot = 2 * ((chip + 4 - d) % 4) + core
        chip_copy(d, slot).wait_recv()
        fwd_copy(d, slot).start()
    sib_copy(sib).wait_recv()
    own_r.wait()
    own_c.wait()
    for d in (2, 1, 3):
        fwd_copy(d, 2 * ((chip + 4 - d) % 4) + 1 - core).wait_recv()
        z_copy(d, (c + 4 - d) % 4).wait_recv()
    for d in (2, 1, 3):
        z_copy(d, c).wait_send()
        chip_copy(d, r).wait_send()
        fwd_copy(d, 2 * ((chip + 4 - d) % 4) + core).wait_send()
    sib_copy(r).wait_send()


def gather(x):
    rows, cols = 8, 4
    dma = pltpu.SemaphoreType.DMA
    return pl.pallas_call(
        gather_kernel,
        out_shape=(
            jax.ShapeDtypeStruct((cols, *x.shape), x.dtype),
            jax.ShapeDtypeStruct((rows, *x.shape), x.dtype),
        ),
        in_specs=[pl.BlockSpec(memory_space=pl.ANY)],
        out_specs=(pl.BlockSpec(memory_space=pl.ANY),) * 2,
        scratch_shapes=[
            dma((2,)), dma((4,)), dma((4,)), dma((4,)), dma((4,)), dma, dma, dma((4,)), dma((4,)),
        ],
        compiler_params=pltpu.CompilerParams(collective_id=0, has_side_effects=True),
        name="gather_vectors",
    )(x)


def apply_kernel(
    slots, tile, per_slab, n_cols, coords, count,
    t_ref, xr_ref, xc_ref, f_ref, m_ref, facc, macc,
):
    step = pl.program_id(0)
    group = t_ref.shape[2]

    @pl.when(step == 0)
    def _():
        facc[...] = jnp.zeros_like(facc)
        macc[...] = jnp.zeros_like(macc)

    def place(s):
        tile_row, tile_col = coords[s], coords[slots + s]
        local = tile_row % (per_slab * n_cols)
        row_at = (local // per_slab, pl.multiple_of(local % per_slab * tile, tile))
        col_at = (
            tile_col // (per_slab * n_cols), pl.multiple_of(tile_col % per_slab * tile, tile),
        )
        return row_at, col_at

    def run(masked):
        made = []
        for g in range(group):
            s = step * group + g
            (ro, rp), (co, cp) = place(s)
            x_row = xr_ref[ro, :, pl.ds(rp, tile)]
            x_col = xc_ref[co, :, pl.ds(cp, tile)]
            upper = lower = t_ref[0, 0, g]
            if masked:
                off = coords[s] != coords[slots + s]
                down = lax.broadcasted_iota(jnp.int32, (tile, tile), 0)
                down = jnp.where(off, -1, down)
                across = lax.broadcasted_iota(jnp.int32, (tile, tile), 1)
                stored = upper.astype(jnp.float32)
                upper = jnp.where(down <= across, stored, 0.0).astype(jnp.bfloat16)
                lower = jnp.where(down < across, stored, 0.0).astype(jnp.bfloat16)
            forward = lax.dot_general(
                x_col, upper, (((1,), (1,)), ((), ())), preferred_element_type=jnp.float32
            )
            mirror = lax.dot_general(
                x_row, lower, (((1,), (0,)), ((), ())), preferred_element_type=jnp.float32
            )
            if masked:
                live = s < count[0]
                forward = jnp.where(live, forward, 0.0)
                mirror = jnp.where(live, mirror, 0.0)
            made.append((forward, mirror))
        for g in range(group):
            (ro, rp), (co, cp) = place(step * group + g)
            forward, mirror = made[g]
            facc[ro, :, pl.ds(rp, tile)] += forward
            macc[co, :, pl.ds(cp, tile)] += mirror

    special = coords[step * group] == coords[slots + step * group]
    for g in range(1, group):
        s = step * group + g
        special = special | (coords[s] == coords[slots + s])
    special = special | (step * group + group > count[0])

    @pl.when(special)
    def _():
        run(True)

    @pl.when(jnp.logical_not(special))
    def _():
        run(False)

    @pl.when(step == pl.num_programs(0) - 1)
    def _():
        f_ref[...] = facc[...].astype(f_ref.dtype)
        m_ref[...] = macc[...].astype(m_ref.dtype)


def apply_tiles(tiles, coords, count, xr, xc, tile):
    slots = tiles.shape[2]
    group = GROUP if slots % GROUP == 0 else 1
    n_cols = xr.shape[0]
    per_slab = xr.shape[2] // tile
    whole = lambda a: pl.BlockSpec(a.shape, lambda i, *_: (0, 0, 0))
    return pl.pallas_call(
        functools.partial(apply_kernel, slots, tile, per_slab, n_cols),
        out_shape=(
            jax.ShapeDtypeStruct(xr.shape, jnp.bfloat16),
            jax.ShapeDtypeStruct(xc.shape, jnp.bfloat16),
        ),
        grid_spec=pltpu.PrefetchScalarGridSpec(
            num_scalar_prefetch=2,
            grid=(slots // group,),
            in_specs=[
                pl.BlockSpec((1, 1, group, tile, tile), lambda i, *_: (0, 0, i, 0, 0)),
                whole(xr),
                whole(xc),
            ],
            out_specs=(whole(xr), whole(xc)),
            scratch_shapes=[
                pltpu.VMEM(xr.shape, jnp.float32),
                pltpu.VMEM(xc.shape, jnp.float32),
            ],
        ),
        compiler_params=pltpu.CompilerParams(vmem_limit_bytes=VMEM_LIMIT),
        name="apply_tiles",
    )(coords, count, tiles, xr, xc)


def scatter_kernel(
    f_ref, m_ref, o_ref, from_sib, chip_out, chip_in, r_out, r_in, l_out, l_in,
    bs, br, cs, cr, rs, rr, ls, lr,
):
    r, c = lax.axis_index("row"), lax.axis_index("col")
    chip, core = r // 2, r % 2
    sib = 2 * chip + 1 - core
    width = o_ref.shape[1]
    piece = width // 8
    f32 = jnp.float32

    barrier = pltpu.get_barrier_semaphore()
    for d in range(1, 4):
        pl.semaphore_signal(
            barrier, inc=1, device_id=(2 * ((chip + d) % 4) + core, c), device_id_type=MESH
        )
    pl.semaphore_signal(barrier, inc=1, device_id=(sib, c), device_id_type=MESH)

    @pl.when(c > 0)
    def _():
        pl.semaphore_signal(barrier, inc=1, device_id=(r, c - 1), device_id_type=MESH)

    @pl.when(c < 3)
    def _():
        pl.semaphore_signal(barrier, inc=1, device_id=(r, c + 1), device_id_type=MESH)

    ends = (c == 0) | (c == 3)

    @pl.when(ends)
    def _():
        pl.semaphore_wait(barrier, 5)

    @pl.when(jnp.logical_not(ends))
    def _():
        pl.semaphore_wait(barrier, 6)

    def right(d, src):
        return pltpu.make_async_remote_copy(
            src, r_in.at[d], rs.at[d], rr.at[d], device_id=(r, c + 1), device_id_type=MESH
        )

    def left(d, src):
        return pltpu.make_async_remote_copy(
            src, l_in.at[d], ls.at[d], lr.at[d], device_id=(r, c - 1), device_id_type=MESH
        )

    def to_sib(d):
        return pltpu.make_async_remote_copy(
            m_ref.at[2 * ((chip + d) % 4) + 1 - core], from_sib.at[d], bs.at[d], br.at[d],
            device_id=(sib, c), device_id_type=MESH,
        )

    def to_chip(d):
        return pltpu.make_async_remote_copy(
            chip_out.at[d], chip_in.at[d], cs.at[d], cr.at[d],
            device_id=(2 * ((chip + d) % 4) + core, c), device_id_type=MESH,
        )

    def add(dst, a, b):
        def body(i, _):
            at = pl.ds(pl.multiple_of(i * piece, piece), piece)
            dst[:, at] = (a[:, at].astype(f32) + b[:, at].astype(f32)).astype(dst.dtype)
            return 0

        lax.fori_loop(0, 8, body, 0)

    for i in range(3):

        @pl.when(c == 0)
        def _():
            right(3 - i, f_ref.at[3 - i]).start()

        @pl.when(c == 3)
        def _():
            left(i, f_ref.at[i]).start()

    for d in (2, 1, 3, 0):
        to_sib(d).start()
    for d in (2, 1, 3):
        to_sib(d).wait_recv()
        add(chip_out.at[d], m_ref.at[2 * ((chip + d) % 4) + core], from_sib.at[d])
        to_chip(d).start()

    for i in range(2):
        d = 3 - i

        @pl.when((c > 0) & (c < d))
        def _():
            right(d, r_out.at[d]).wait_recv()
            add(r_out.at[d], f_ref.at[d], r_in.at[d])
            right(d, r_out.at[d]).start()

        e = i

        @pl.when((c < 3) & (c > e))
        def _():
            left(e, l_out.at[e]).wait_recv()
            add(l_out.at[e], f_ref.at[e], l_in.at[e])
            left(e, l_out.at[e]).start()

    to_sib(0).wait_recv()
    for d in (2, 1, 3):
        to_chip(d).wait_recv()

    def first(i, _):
        at = pl.ds(pl.multiple_of(i * piece, piece), piece)
        total = f_ref[c, :, at].astype(f32) + m_ref[r, :, at].astype(f32)
        total = total + from_sib[0, :, at].astype(f32)
        for d in (2, 1, 3):
            total = total + chip_in[d, :, at].astype(f32)
        o_ref[:, at] = total
        return 0

    lax.fori_loop(0, 8, first, 0)

    @pl.when(c > 0)
    def _():
        right(c, r_out.at[c]).wait_recv()
        add(o_ref, o_ref, r_in.at[c])

    @pl.when(c < 3)
    def _():
        left(c, l_out.at[c]).wait_recv()
        add(o_ref, o_ref, l_in.at[c])

    for d in range(4):
        to_sib(d).wait_send()
    for d in (2, 1, 3):
        to_chip(d).wait_send()
    for i in range(3):

        @pl.when(c < 3 - i)
        def _():
            right(3 - i, r_out.at[3 - i]).wait_send()

        @pl.when(c > i)
        def _():
            left(i, l_out.at[i]).wait_send()


def scatter(f, m):
    dma = pltpu.SemaphoreType.DMA
    block = pltpu.VMEM((4, *f.shape[1:]), f.dtype)
    return pl.pallas_call(
        scatter_kernel,
        out_shape=jax.ShapeDtypeStruct(f.shape[1:], jnp.float32),
        in_specs=[pl.BlockSpec(memory_space=pltpu.VMEM)] * 2,
        out_specs=pl.BlockSpec(memory_space=pltpu.VMEM),
        scratch_shapes=[block] * 7 + [dma((4,))] * 8,
        compiler_params=pltpu.CompilerParams(
            collective_id=1, has_side_effects=True, vmem_limit_bytes=VMEM_LIMIT
        ),
        name="scatter_products",
    )(f, m)


def shards(n_rows, n_cols, tiles, tile_coords, tile_counts, vectors):
    tile = tiles.shape[-1]
    x = vectors.T
    coords, count = tile_coords.reshape(-1), tile_counts.reshape(-1)
    direct = (n_rows, n_cols) == (8, 4)
    if direct:
        xr, xc = gather(x)
    else:
        xr = lax.all_gather(x, "col", axis=0)
        xc = lax.all_gather(x, "row", axis=0)
    f, m = apply_tiles(tiles, coords, count, xr, xc, tile)
    if direct:
        product = scatter(f, m)
    else:
        f = lax.all_to_all(f, "col", 0, 0, tiled=True)
        m = lax.all_to_all(m, "row", 0, 0, tiled=True)
        product = jnp.sum(f.astype(jnp.float32), 0) + jnp.sum(m.astype(jnp.float32), 0)
    return product.T


def solution(mesh):
    in_specs = (
        P("row", "col", None, None, None),
        P(None, "row", "col", None),
        P("row", "col"),
        P(("row", "col"), None),
    )
    out_specs = P(("row", "col"), None)
    body = functools.partial(shards, mesh.shape["row"], mesh.shape["col"])
    return jax.shard_map(body, mesh=mesh, in_specs=in_specs, out_specs=out_specs, check_vma=False)
```

time: 184 us -> 72.8 us (0.40)
  waiting for transfers between devices: 115 us -> 0 us
  Pallas kernels: 0 us -> 67.9 us
  matrix products: 18.5 us -> 0 us
  blocking collectives: 15.9 us -> 0 us
  between operations: 15.3 us -> 0.69 us
  local copies, waits for them, and re-layouts: 17 us -> 2.61 us
    all_gather x4 -> x0, waiting for transfers between devices: 114 us -> none  [the longest x1 39.2 us: shards(): lax.all_gather(mirror, 'row', axis=0, tiled=True)]
    pallas_call x0 -> x3, Pallas kernels: none -> 67.9 us  [the longest x1 30.7 us: scatter(): pl.pallas_call(scatter_kernel, out_shape=jax.ShapeDtypeStruct(f.shape[1:]...]
    dot_general x4 -> x0, matrix products: 18.5 us -> none  [the longest x1 6.91 us: shards(): jnp.einsum('tab,tbv->tav', upper_part, col_group[col_local], preferred_el...]
    unnamed x2 -> x0, blocking collectives: 15.9 us -> none
    add x2 -> x0, local copies, waits for them, and re-layouts: 6.27 us -> none  [shards(): return owned_direct + owned_reflected]
    reshape x4 -> x1, local copies, waits for them, and re-layouts: 5.62 us -> 0.08 us  [shards(): coords, count = (tile_coords.reshape(-1), tile_counts.reshape(-1))]
    select_n x2 -> x0, local copies, waits for them, and re-layouts: 2.58 us -> none  [the longest x1 1.29 us: shards(): jnp.where(live_slots[:, None, None], apply_operator, zero_val)]
  transfers between devices with their start and end apart: 4 -> 0, of which waited for: 4 -> 0; matrix products, arithmetic and copies ran while one was open for 15% -> 0% of each run, Pallas kernels for 0% -> 0%
where the time goes in v1:
time: 72.8 us; the launch traced here: 72.5 us
  Pallas kernels  67.9 us (93%)
  local copies, waits for them, and re-layouts  2.61 us (4%)
  other arithmetic  1.34 us (2%)
    pallas_call x1, Pallas kernels, scatter(): pl.pallas_call(scatter_kernel, out_shape=jax.ShapeDtypeStruct(f.shape[1:]...  30.7 us
    pallas_call x1, Pallas kernels, gather(): pl.pallas_call(gather_kernel, out_shape=(jax.ShapeDtypeStruct((cols, *x.s...  25.5 us
    pallas_call x1, Pallas kernels, apply_tiles(): pl.pallas_call(functools.partial(apply_kernel, slots, tile, per_slab, n_c...  11.7 us
    unnamed x4, local copies, waits for them, and re-layouts  2.53 us

profile of v1, /device:TPU:0, one launch (start us, length us, event | category | flops | bytes accessed | tf_op | source)
XLA Modules:
  0.0 72.5 jit_solution(16975054090277689854)
XLA Ops:
  0.7 0.5 broadcast.3
  1.2 1.3 %reduce.3 = s32[2,80]{1,0:T(2,128)S(1)} reduce(s32[2,1,1,80]{3,2,1,0:T(1,128)} %param.5, s32[]{:T(128)} %broadcast.3), dimensions={1,2}, to_apply=%param.5.reduce_sub_computation.3 | reduce | bytes 1284 | tf_op args[1]
  2.5 0.1 reshape.6.coords
  2.6 25.5 %gather_vectors.1 = (bf16[4,16,8192]{2,1,0:T(8,128)(2,1)}, bf16[8,16,8192]{2,1,0:T(8,128)(2,1)}) custom-call(bf16[16,8192]{1,0:T(8,128)(2,1)} %bitcast.5), custom_call_target="tpu_custom_call" | custom-call | tf_op jit(solution)/shard_map/gather_vectors/pallas_call | solution.py:82
  28.1 0.0 copy-start
  28.1 1.2 %copy-done = bf16[4,16,8192]{2,1,0:T(8,128)(2,1)S(1)} copy-done((bf16[4,16,8192]{2,1,0:T(8,128)(2,1)S(1)}, bf16[4,16,8192]{2,1,0:T(8,128)(2,1)}, u32[]{:S(2)}) %copy-start) | copy-done | bytes 1048600
  29.3 11.7 %apply_tiles.1 = (bf16[4,16,8192]{2,1,0:T(8,128)(2,1)S(1)}, bf16[8,16,8192]{2,1,0:T(8,128)(2,1)S(1)}) custom-call(s32[160]{0:T(256)S(1)} %reshape.6.coords, s32[1]{0:T(128)} %bitcast.3.count, bf16[1,1,80,256,256]{4,3,2,1,0:T(8,128)(2,1)} %t_ref.1, bf16[4,16,8192]{2,1,0:T(8,128)(2,1)S(1)} %copy-done, bf16[8,16,8192]{2,1,0:T(8,128)(2,1)} %get-tuple-element.10.xc_ref), custom_call_target="tpu_custom_call" | custom-call | tf_op jit(solution)/shard_map/apply_tiles/pallas_call | solution.py:178
  41.0 30.7 %scatter_products.1 = f32[16,8192]{1,0:T(8,128)S(1)} custom-call(bf16[4,16,8192]{2,1,0:T(8,128)(2,1)S(1)} %get-tuple-element.11.f_ref, bf16[8,16,8192]{2,1,0:T(8,128)(2,1)S(1)} %get-tuple-element.12.m_ref), custom_call_target="tpu_custom_call" | custom-call | tf_op jit(solution)/shard_map/scatter_products/pallas_call | solution.py:346
  71.7 0.8 %copy.7 = f32[8192,16]{0,1:T(8,128)} copy(f32[8192,16]{0,1:T(8,128)S(1)} %bitcast.4) | data formatting | bytes 1048576
Async XLA Ops:
  28.1 1.2 %copy-start = (bf16[4,16,8192]{2,1,0:T(8,128)(2,1)S(1)}, bf16[4,16,8192]{2,1,0:T(8,128)(2,1)}, u32[]{:S(2)}) copy-start(bf16[4,16,8192]{2,1,0:T(8,128)(2,1)} %get-tuple-element.9.xr_ref) | copy-start | bytes 3145732

commit v2 on v1

v2 whole, which is shorter than its diff:
```python
import functools

import jax
import jax.numpy as jnp
from jax import lax
from jax.experimental import pallas as pl
from jax.experimental.pallas import tpu as pltpu
from jax.sharding import PartitionSpec as P

MESH = pl.DeviceIdType.MESH
VMEM_LIMIT = 48 * 1024 * 1024
GROUP = 8


def fused_kernel(
    coords, count, coords_v, x_ref, t_ref, o_ref,
    mine, xr, xc, upper, lower, tri, made, keys, onehot, f_ref, m_ref,
    from_sib, chip_out, chip_in, r_out, r_in, l_out, l_in,
    tile_sem, own_sem, zs, zr, gs, gr, ss, sr, fs, fr, bs, br, cs, cr, rs, rr, ls, lr,
):
    r, c = lax.axis_index("row"), lax.axis_index("col")
    chip, core = r // 2, r % 2
    sib = 2 * chip + 1 - core
    slots, tile = upper.shape[0], upper.shape[1]
    vecs, width = x_ref.shape
    per_slab = width // tile
    groups = slots // GROUP
    f32, bf16, i32 = jnp.float32, jnp.bfloat16, jnp.int32

    for p in range(per_slab):
        mine[p] = x_ref[:, p * tile : (p + 1) * tile]

    def slab(i):
        return pl.ds(i * per_slab, per_slab)

    def chip_at(d):
        return (chip + d) % 4

    def tile_copy(g):
        at = pl.ds(g * GROUP, GROUP)
        return pltpu.make_async_copy(t_ref.at[0, 0, at], lower.at[at], tile_sem.at[g])

    barrier = pltpu.get_barrier_semaphore()
    for d in range(1, 4):
        pl.semaphore_signal(barrier, inc=1, device_id=(r, (c + d) % 4), device_id_type=MESH)
        pl.semaphore_signal(
            barrier, inc=1, device_id=(2 * chip_at(d) + core, c), device_id_type=MESH
        )
    pl.semaphore_signal(barrier, inc=1, device_id=(sib, c), device_id_type=MESH)
    pl.semaphore_wait(barrier, 7)

    def remote(src, dst, send, recv, row, col):
        return pltpu.make_async_remote_copy(
            src, dst, send, recv, device_id=(row, col), device_id_type=MESH
        )

    def z_copy(d, slot):
        return remote(mine, xr.at[slab(slot)], zs.at[d], zr.at[d], r, (c + d) % 4)

    def chip_copy(d, slot):
        return remote(mine, xc.at[slab(slot)], gs.at[d], gr.at[d], 2 * chip_at(d) + core, c)

    def sib_copy(slot):
        return remote(mine, xc.at[slab(slot)], ss, sr, sib, c)

    def fwd_copy(d, slot):
        return remote(xc.at[slab(slot)], xc.at[slab(slot)], fs.at[d], fr.at[d], sib, c)

    def right(d, src):
        return remote(src, r_in.at[d], rs.at[d], rr.at[d], r, c + 1)

    def left(d, src):
        return remote(src, l_in.at[d], ls.at[d], lr.at[d], r, c - 1)

    def to_sib(d):
        return remote(
            m_ref.at[2 * chip_at(d) + 1 - core], from_sib.at[d], bs.at[d], br.at[d], sib, c
        )

    def to_chip(d):
        return remote(
            chip_out.at[d], chip_in.at[d], cs.at[d], cr.at[d], 2 * chip_at(d) + core, c
        )

    for d in (2, 1, 3):
        chip_copy(d, r).start()
        z_copy(d, c).start()
    sib_copy(r).start()
    own_r = pltpu.make_async_copy(mine, xr.at[slab(c)], own_sem.at[0])
    own_c = pltpu.make_async_copy(mine, xc.at[slab(r)], own_sem.at[1])
    own_r.start()
    own_c.start()

    def start_tiles(g, _):
        tile_copy(g).start()
        return 0

    lax.fori_loop(0, groups, start_tiles, 0)

    tile_row, tile_col = coords_v[0, 0], coords_v[1, 0]
    live = lax.broadcasted_iota(i32, (1, slots), 1) < count[0, 0]
    span = 4 * per_slab
    places = (tile_row % span, tile_col // span * per_slab + tile_col % per_slab)
    wide = slots * vecs
    spread = lax.broadcasted_iota(i32, (slots, wide), 1) // vecs
    spread = (spread == lax.broadcasted_iota(i32, (slots, wide), 0)).astype(f32).astype(bf16)
    across = lax.broadcasted_iota(i32, (vecs, wide), 1) % vecs
    same = across == lax.broadcasted_iota(i32, (vecs, wide), 0)
    for k in range(2):
        place = jnp.where(live, places[k], -1).astype(f32)
        place = jnp.broadcast_to(place, (vecs, slots)).astype(bf16)
        place = jnp.dot(place, spread, preferred_element_type=f32)
        keys[k] = jnp.where(same, place, -1.0)

    down = lax.broadcasted_iota(i32, (tile, tile), 0)
    over = lax.broadcasted_iota(i32, (tile, tile), 1)
    tri[0] = (down <= over).astype(f32).astype(bf16)
    tri[1] = (down < over).astype(f32).astype(bf16)

    def split_group(g, _):
        tile_copy(g).wait()
        for i in range(GROUP):
            s = g * GROUP + i
            gap = jnp.full((1, tile), coords[0, 0, 0, s] - coords[1, 0, 0, s], i32)
            off = jnp.minimum(gap * gap, 1).astype(f32).astype(bf16)
            stored = lower[s]
            upper[s] = stored * jnp.maximum(tri[0], off)
            lower[s] = stored * jnp.maximum(tri[1], off)
        return 0

    lax.fori_loop(0, groups, split_group, 0)

    for d in (2, 1, 3):
        slot = 2 * ((chip + 4 - d) % 4) + core
        chip_copy(d, slot).wait_recv()
        fwd_copy(d, slot).start()
    sib_copy(sib).wait_recv()
    own_c.wait()
    for d in (2, 1, 3):
        fwd_copy(d, 2 * ((chip + 4 - d) % 4) + 1 - core).wait_recv()

    def forward_group(g, _):
        outs = []
        for i in range(GROUP):
            s = g * GROUP + i
            col = coords[1, 0, 0, s]
            at = lax.div(col, span) * per_slab + lax.rem(col, per_slab)
            outs.append(
                lax.dot_general(
                    xc[at], upper[s], (((1,), (1,)), ((), ())),
                    preferred_element_type=f32,
                ).astype(bf16)
            )
        rows = pl.ds(pl.multiple_of(g * GROUP * vecs, GROUP * vecs), GROUP * vecs)
        made[rows, :] = jnp.concatenate(outs, axis=0)
        return 0

    def mirror_group(g, _):
        outs = []
        for i in range(GROUP):
            s = g * GROUP + i
            row = lax.rem(coords[0, 0, 0, s], span)
            outs.append(
                jnp.dot(xr[row], lower[s], preferred_element_type=f32).astype(bf16)
            )
        rows = pl.ds(pl.multiple_of(g * GROUP * vecs, GROUP * vecs), GROUP * vecs)
        made[rows, :] = jnp.concatenate(outs, axis=0)
        return 0

    def combine(k, owner, dst):
        def pick(p, _):
            rows = pl.ds(pl.multiple_of(p * vecs, vecs), vecs)
            wanted = (owner * per_slab + p).astype(f32)
            onehot[rows, :] = jnp.where(keys[k] == wanted, 1.0, 0.0).astype(bf16)
            return 0

        lax.fori_loop(0, per_slab, pick, 0, unroll=4)
        dst[owner] = jnp.dot(onehot[...], made[...], preferred_element_type=f32).astype(bf16)

    def add(dst, a, b):
        dst[...] = (a[...].astype(f32) + b[...].astype(f32)).astype(dst.dtype)

    def chain(i):
        d, e = 3 - i, i

        @pl.when((c > 0) & (c < d))
        def _():
            right(d, r_out.at[d]).wait_recv()
            add(r_out.at[d], f_ref.at[d], r_in.at[d])
            right(d, r_out.at[d]).start()

        @pl.when((c < 3) & (c > e))
        def _():
            left(e, l_out.at[e]).wait_recv()
            add(l_out.at[e], f_ref.at[e], l_in.at[e])
            left(e, l_out.at[e]).start()

    lax.fori_loop(0, groups, forward_group, 0)

    def combine_f(d, _):
        combine(0, d, f_ref)
        return 0

    lax.fori_loop(0, 4, combine_f, 0)
    for i in range(3):

        @pl.when(c == 0)
        def _():
            right(3 - i, f_ref.at[3 - i]).start()

        @pl.when(c == 3)
        def _():
            left(i, f_ref.at[i]).start()

    own_r.wait()
    for d in (2, 1, 3):
        z_copy(d, (c + 4 - d) % 4).wait_recv()
    lax.fori_loop(0, groups, mirror_group, 0)
    chain(0)

    def combine_theirs(j, _):
        combine(1, 2 * ((chip + 1 + j) % 4) + 1 - core, m_ref)
        to_sib((1 + j) % 4).start()
        return 0

    lax.fori_loop(0, 4, combine_theirs, 0)

    def combine_ours(j, _):
        combine(1, 2 * ((chip + 1 + j) % 4) + core, m_ref)
        return 0

    lax.fori_loop(0, 4, combine_ours, 0)
    for d in (1, 2, 3):
        to_sib(d).wait_recv()
        add(chip_out.at[d], m_ref.at[2 * chip_at(d) + core], from_sib.at[d])
        to_chip(d).start()
    chain(1)
    to_sib(0).wait_recv()
    for d in (1, 2, 3):
        to_chip(d).wait_recv()

    def rows_of(p):
        rows = pl.ds(pl.multiple_of(p * vecs, vecs), vecs)
        return rows, pl.ds(pl.multiple_of(p * tile, tile), tile)

    def total(p, _):
        rows, at = rows_of(p)
        out = f_ref[c, rows, :].astype(f32) + m_ref[r, rows, :].astype(f32)
        out = out + from_sib[0, rows, :].astype(f32)
        for d in (1, 2, 3):
            out = out + chip_in[d, rows, :].astype(f32)
        o_ref[:, at] = out
        return 0

    lax.fori_loop(0, per_slab, total, 0, unroll=4)

    def last(src):
        def body(p, _):
            rows, at = rows_of(p)
            o_ref[:, at] = o_ref[:, at] + src[c, rows, :].astype(f32)
            return 0

        lax.fori_loop(0, per_slab, body, 0, unroll=4)

    @pl.when(c > 0)
    def _():
        right(c, r_out.at[c]).wait_recv()
        last(r_in)

    @pl.when(c < 3)
    def _():
        left(c, l_out.at[c]).wait_recv()
        last(l_in)

    for d in (1, 2, 3):
        z_copy(d, c).wait_send()
        chip_copy(d, r).wait_send()
        fwd_copy(d, 2 * ((chip + 4 - d) % 4) + core).wait_send()
        to_chip(d).wait_send()
    sib_copy(r).wait_send()
    for d in range(4):
        to_sib(d).wait_send()
    for i in range(3):

        @pl.when(c < 3 - i)
        def _():
            right(3 - i, r_out.at[3 - i]).wait_send()

        @pl.when(c > i)
        def _():
            left(i, l_out.at[i]).wait_send()


def fused(tiles, tile_coords, tile_counts, x):
    slots, tile = tiles.shape[2], tiles.shape[-1]
    vecs, width = x.shape
    slab = width // tile
    rows = slab * vecs
    dma, bf16 = pltpu.SemaphoreType.DMA, jnp.bfloat16
    block = pltpu.VMEM((4, rows, tile), bf16)
    return pl.pallas_call(
        fused_kernel,
        out_shape=jax.ShapeDtypeStruct(x.shape, jnp.float32),
        in_specs=[
            pl.BlockSpec(memory_space=pltpu.SMEM),
            pl.BlockSpec(memory_space=pltpu.SMEM),
            pl.BlockSpec(memory_space=pltpu.VMEM),
            pl.BlockSpec(memory_space=pltpu.VMEM),
            pl.BlockSpec(memory_space=pl.ANY),
        ],
        out_specs=pl.BlockSpec(memory_space=pltpu.VMEM),
        scratch_shapes=[
            pltpu.VMEM((slab, vecs, tile), bf16),
            pltpu.VMEM((4 * slab, vecs, tile), bf16),
            pltpu.VMEM((8 * slab, vecs, tile), bf16),
            pltpu.VMEM((slots, tile, tile), bf16),
            pltpu.VMEM((slots, tile, tile), bf16),
            pltpu.VMEM((2, tile, tile), bf16),
            pltpu.VMEM((slots * vecs, tile), bf16),
            pltpu.VMEM((2, vecs, slots * vecs), jnp.float32),
            pltpu.VMEM((rows, slots * vecs), bf16),
            block,
            pltpu.VMEM((8, rows, tile), bf16),
            *[block] * 7,
            dma((slots // GROUP,)),
            dma((2,)),
            *[dma((4,))] * 4,
            *[dma] * 2,
            *[dma((4,))] * 10,
        ],
        compiler_params=pltpu.CompilerParams(
            collective_id=0, has_side_effects=True, vmem_limit_bytes=VMEM_LIMIT
        ),
        name="fused_product",
    )(tile_coords, tile_counts, tile_coords, x, tiles)


def apply_kernel(
    slots, tile, per_slab, n_cols, coords, count,
    t_ref, xr_ref, xc_ref, f_ref, m_ref, facc, macc,
):
    step = pl.program_id(0)
    group = t_ref.shape[2]

    @pl.when(step == 0)
    def _():
        facc[...] = jnp.zeros_like(facc)
        macc[...] = jnp.zeros_like(macc)

    def place(s):
        tile_row, tile_col = coords[s], coords[slots + s]
        local = tile_row % (per_slab * n_cols)
        row_at = (local // per_slab, pl.multiple_of(local % per_slab * tile, tile))
        col_at = (
            tile_col // (per_slab * n_cols), pl.multiple_of(tile_col % per_slab * tile, tile),
        )
        return row_at, col_at

    def run(masked):
        made = []
        for g in range(group):
            s = step * group + g
            (ro, rp), (co, cp) = place(s)
            x_row = xr_ref[ro, :, pl.ds(rp, tile)]
            x_col = xc_ref[co, :, pl.ds(cp, tile)]
            upper = lower = t_ref[0, 0, g]
            if masked:
                off = coords[s] != coords[slots + s]
                down = lax.broadcasted_iota(jnp.int32, (tile, tile), 0)
                down = jnp.where(off, -1, down)
                across = lax.broadcasted_iota(jnp.int32, (tile, tile), 1)
                stored = upper.astype(jnp.float32)
                upper = jnp.where(down <= across, stored, 0.0).astype(jnp.bfloat16)
                lower = jnp.where(down < across, stored, 0.0).astype(jnp.bfloat16)
            forward = lax.dot_general(
                x_col, upper, (((1,), (1,)), ((), ())), preferred_element_type=jnp.float32
            )
            mirror = lax.dot_general(
                x_row, lower, (((1,), (0,)), ((), ())), preferred_element_type=jnp.float32
            )
            if masked:
                live = s < count[0]
                forward = jnp.where(live, forward, 0.0)
                mirror = jnp.where(live, mirror, 0.0)
            made.append((forward, mirror))
        for g in range(group):
            (ro, rp), (co, cp) = place(step * group + g)
            forward, mirror = made[g]
            facc[ro, :, pl.ds(rp, tile)] += forward
            macc[co, :, pl.ds(cp, tile)] += mirror

    special = coords[step * group] == coords[slots + step * group]
    for g in range(1, group):
        s = step * group + g
        special = special | (coords[s] == coords[slots + s])
    special = special | (step * group + group > count[0])

    @pl.when(special)
    def _():
        run(True)

    @pl.when(jnp.logical_not(special))
    def _():
        run(False)

    @pl.when(step == pl.num_programs(0) - 1)
    def _():
        f_ref[...] = facc[...].astype(f_ref.dtype)
        m_ref[...] = macc[...].astype(m_ref.dtype)


def apply_tiles(tiles, coords, count, xr, xc, tile):
    slots = tiles.shape[2]
    group = GROUP if slots % GROUP == 0 else 1
    n_cols = xr.shape[0]
    per_slab = xr.shape[2] // tile
    whole = lambda a: pl.BlockSpec(a.shape, lambda i, *_: (0, 0, 0))
    return pl.pallas_call(
        functools.partial(apply_kernel, slots, tile, per_slab, n_cols),
        out_shape=(
            jax.ShapeDtypeStruct(xr.shape, jnp.bfloat16),
            jax.ShapeDtypeStruct(xc.shape, jnp.bfloat16),
        ),
        grid_spec=pltpu.PrefetchScalarGridSpec(
            num_scalar_prefetch=2,
            grid=(slots // group,),
            in_specs=[
                pl.BlockSpec((1, 1, group, tile, tile), lambda i, *_: (0, 0, i, 0, 0)),
                whole(xr),
                whole(xc),
            ],
            out_specs=(whole(xr), whole(xc)),
            scratch_shapes=[
                pltpu.VMEM(xr.shape, jnp.float32),
                pltpu.VMEM(xc.shape, jnp.float32),
            ],
        ),
        compiler_params=pltpu.CompilerParams(vmem_limit_bytes=VMEM_LIMIT),
        name="apply_tiles",
    )(coords, count, tiles, xr, xc)


def shards(n_rows, n_cols, tiles, tile_coords, tile_counts, vectors):
    tile = tiles.shape[-1]
    x = vectors.T
    if (n_rows, n_cols) == (8, 4):
        return fused(tiles, tile_coords, tile_counts, x).T
    coords, count = tile_coords.reshape(-1), tile_counts.reshape(-1)
    xr = lax.all_gather(x, "col", axis=0)
    xc = lax.all_gather(x, "row", axis=0)
    f, m = apply_tiles(tiles, coords, count, xr, xc, tile)
    f = lax.all_to_all(f, "col", 0, 0, tiled=True)
    m = lax.all_to_all(m, "row", 0, 0, tiled=True)
    return (jnp.sum(f.astype(jnp.float32), 0) + jnp.sum(m.astype(jnp.float32), 0)).T


def solution(mesh):
    in_specs = (
        P("row", "col", None, None, None),
        P(None, "row", "col", None),
        P("row", "col"),
        P(("row", "col"), None),
    )
    out_specs = P(("row", "col"), None)
    body = functools.partial(shards, mesh.shape["row"], mesh.shape["col"])
    return jax.shard_map(body, mesh=mesh, in_specs=in_specs, out_specs=out_specs, check_vma=False)
```

time: 72.8 us -> 71.3 us (0.979)
  the two profiles are of different devices: /device:TPU:0 before, /device:TPU:9 now
where the time goes in v2:
time: 71.3 us; the launch traced here: 71.2 us
  Pallas kernels  68.1 us (96%)
  local copies, waits for them, and re-layouts  2.42 us (3%)
    pallas_call x1, Pallas kernels, fused(): pl.pallas_call(fused_kernel, out_shape=jax.ShapeDtypeStruct(x.shape, jnp....  68.1 us
    unnamed x5, local copies, waits for them, and re-layouts  2.42 us

profile of v2, /device:TPU:9, one launch (start us, length us, event | category | flops | bytes accessed | tf_op | source)
XLA Modules:
  0.0 71.2 jit_solution(17425215767179482210)
XLA Ops:
  0.7 0.0 copy-start
  0.7 0.9 %copy-done = bf16[8192,16]{0,1:T(8,128)(2,1)S(1)} copy-done((bf16[8192,16]{0,1:T(8,128)(2,1)S(1)}, bf16[8192,16]{0,1:T(8,128)(2,1)}, u32[]{:S(2)}) %copy-start) | copy-done | bytes 262168
  1.6 0.0 copy-start.1
  1.6 0.7 copy-done.1
  2.3 68.1 %fused_product.1 = f32[16,8192]{1,0:T(8,128)S(1)} custom-call(s32[2,1,1,80]{3,2,1,0:T(1,128)S(1)} %copy-done.1, s32[1,1]{1,0:T(1,128)S(6)} %copy.6.count, s32[2,1,1,80]{3,2,1,0:T(1,128)S(1)} %copy-done.1, bf16[16,8192]{1,0:T(8,128)(2,1)S(1)} %bitcast.3, bf16[1,1,80,256,256]{4,3,2,1,0:T(8,128)(2,1)} %t_ref.1), custom_call_target="tpu_custom_call" | custom-call | tf_op jit(solution)/shard_map/fused_product/pallas_call | solution.py:301
  70.4 0.8 %copy.7 = f32[8192,16]{0,1:T(8,128)} copy(f32[8192,16]{0,1:T(8,128)S(1)} %bitcast.2) | data formatting | bytes 1048576
Async XLA Ops:
  0.7 1.0 %copy-start = (bf16[8192,16]{0,1:T(8,128)(2,1)S(1)}, bf16[8192,16]{0,1:T(8,128)(2,1)}, u32[]{:S(2)}) copy-start(bf16[8192,16]{0,1:T(8,128)(2,1)} %param.7) | copy-start | bytes 786436
  1.6 0.7 copy-start.1

commit v3 on v2

--- a/solution.py
+++ b/solution.py
@@ -180,16 +180,14 @@
     def add(dst, a, b):
         dst[...] = (a[...].astype(f32) + b[...].astype(f32)).astype(dst.dtype)
 
-    def chain(i):
-        d, e = 3 - i, i
-
-        @pl.when((c > 0) & (c < d))
+    def chain(at_right, d, at_left, e):
+        @pl.when(c == at_right)
         def _():
             right(d, r_out.at[d]).wait_recv()
             add(r_out.at[d], f_ref.at[d], r_in.at[d])
             right(d, r_out.at[d]).start()
 
-        @pl.when((c < 3) & (c > e))
+        @pl.when(c == at_left)
         def _():
             left(e, l_out.at[e]).wait_recv()
             add(l_out.at[e], f_ref.at[e], l_in.at[e])
@@ -216,7 +214,7 @@
     for d in (2, 1, 3):
         z_copy(d, (c + 4 - d) % 4).wait_recv()
     lax.fori_loop(0, groups, mirror_group, 0)
-    chain(0)
+    chain(1, 3, 2, 0)
 
     def combine_theirs(j, _):
         combine(1, 2 * ((chip + 1 + j) % 4) + 1 - core, m_ref)
@@ -225,16 +223,15 @@
 
     lax.fori_loop(0, 4, combine_theirs, 0)
 
-    def combine_ours(j, _):
-        combine(1, 2 * ((chip + 1 + j) % 4) + core, m_ref)
-        return 0
-
-    lax.fori_loop(0, 4, combine_ours, 0)
     for d in (1, 2, 3):
+        combine(1, 2 * chip_at(d) + core, m_ref)
         to_sib(d).wait_recv()
         add(chip_out.at[d], m_ref.at[2 * chip_at(d) + core], from_sib.at[d])
         to_chip(d).start()
-    chain(1)
+        if d == 1:
+            chain(1, 2, 2, 1)
+    chain(2, 3, 1, 0)
+    combine(1, r, m_ref)
     to_sib(0).wait_recv()
     for d in (1, 2, 3):
         to_chip(d).wait_recv()

time: 71.3 us -> 55.8 us (0.78)
  the two profiles are of different devices: /device:TPU:9 before, /device:TPU:0 now
where the time goes in v3:
time: 55.8 us; the launch traced here: 54.9 us
  Pallas kernels  51.8 us (93%)
  local copies, waits for them, and re-layouts  2.42 us (4%)
  between operations  0.67 us (1%)
    pallas_call x1, Pallas kernels, fused(): pl.pallas_call(fused_kernel, out_shape=jax.ShapeDtypeStruct(x.shape, jnp....  51.8 us
    unnamed x5, local copies, waits for them, and re-layouts  2.42 us

profile of v3, /device:TPU:0, one launch (start us, length us, event | category | flops | bytes accessed | tf_op | source)
XLA Modules:
  0.0 54.9 jit_solution(1797182257462383122)
XLA Ops:
  0.7 0.0 copy-start
  0.7 0.9 %copy-done = bf16[8192,16]{0,1:T(8,128)(2,1)S(1)} copy-done((bf16[8192,16]{0,1:T(8,128)(2,1)S(1)}, bf16[8192,16]{0,1:T(8,128)(2,1)}, u32[]{:S(2)}) %copy-start) | copy-done | bytes 262168
  1.6 0.0 copy-start.1
  1.6 0.7 %copy-done.1 = s32[2,1,1,80]{3,2,1,0:T(1,128)S(1)} copy-done((s32[2,1,1,80]{3,2,1,0:T(1,128)S(1)}, s32[2,1,1,80]{3,2,1,0:T(1,128)}, u32[]{:S(2)}) %copy-start.1) | copy-done | bytes 664
  2.3 51.8 %fused_product.1 = f32[16,8192]{1,0:T(8,128)S(1)} custom-call(s32[2,1,1,80]{3,2,1,0:T(1,128)S(1)} %copy-done.1, s32[1,1]{1,0:T(1,128)S(6)} %copy.6.count, s32[2,1,1,80]{3,2,1,0:T(1,128)S(1)} %copy-done.1, bf16[16,8192]{1,0:T(8,128)(2,1)S(1)} %bitcast.3, bf16[1,1,80,256,256]{4,3,2,1,0:T(8,128)(2,1)} %t_ref.1), custom_call_target="tpu_custom_call" | custom-call | tf_op jit(solution)/shard_map/fused_product/pallas_call | solution.py:298
  54.1 0.8 %copy.7 = f32[8192,16]{0,1:T(8,128)} copy(f32[8192,16]{0,1:T(8,128)S(1)} %bitcast.2) | data formatting | bytes 1048576
Async XLA Ops:
  0.7 1.0 %copy-start = (bf16[8192,16]{0,1:T(8,128)(2,1)S(1)}, bf16[8192,16]{0,1:T(8,128)(2,1)}, u32[]{:S(2)}) copy-start(bf16[8192,16]{0,1:T(8,128)(2,1)} %param.7) | copy-start | bytes 786436
  1.6 0.7 %copy-start.1 = (s32[2,1,1,80]{3,2,1,0:T(1,128)S(1)}, s32[2,1,1,80]{3,2,1,0:T(1,128)}, u32[]{:S(2)}) copy-start(s32[2,1,1,80]{3,2,1,0:T(1,128)} %coords_v.1) | copy-start | bytes 1924

commit v4 on v3

--- a/solution.py
+++ b/solution.py
@@ -195,12 +195,11 @@
 
     lax.fori_loop(0, groups, forward_group, 0)
 
-    def combine_f(d, _):
-        combine(0, d, f_ref)
-        return 0
-
-    lax.fori_loop(0, 4, combine_f, 0)
-    for i in range(3):
+    half = c // 2
+    for i in range(4):
+        combine(0, (3 - i) * (1 - half) + i * half, f_ref)
+        if i == 3:
+            break
 
         @pl.when(c == 0)
         def _():

time: 55.8 us -> 53.8 us (0.964)
  Pallas kernels: 51.8 us -> 49.7 us
    pallas_call x1, Pallas kernels: 51.8 us -> 49.7 us  [fused(): pl.pallas_call(fused_kernel, out_shape=jax.ShapeDtypeStruct(x.shape, jnp....]
where the time goes in v4:
time: 53.8 us; the launch traced here: 52.8 us
  Pallas kernels  49.7 us (92%)
  local copies, waits for them, and re-layouts  2.42 us (4%)
  between operations  0.67 us (1%)
    pallas_call x1, Pallas kernels, fused(): pl.pallas_call(fused_kernel, out_shape=jax.ShapeDtypeStruct(x.shape, jnp....  49.7 us
    unnamed x5, local copies, waits for them, and re-layouts  2.42 us

profile of v4, /device:TPU:0, one launch (start us, length us, event | category | flops | bytes accessed | tf_op | source)
XLA Modules:
  0.0 52.8 jit_solution(12007965005509470989)
XLA Ops:
  0.7 0.0 copy-start
  0.7 0.9 %copy-done = bf16[8192,16]{0,1:T(8,128)(2,1)S(1)} copy-done((bf16[8192,16]{0,1:T(8,128)(2,1)S(1)}, bf16[8192,16]{0,1:T(8,128)(2,1)}, u32[]{:S(2)}) %copy-start) | copy-done | bytes 262168
  1.6 0.0 copy-start.1
  1.6 0.7 %copy-done.1 = s32[2,1,1,80]{3,2,1,0:T(1,128)S(1)} copy-done((s32[2,1,1,80]{3,2,1,0:T(1,128)S(1)}, s32[2,1,1,80]{3,2,1,0:T(1,128)}, u32[]{:S(2)}) %copy-start.1) | copy-done | bytes 664
  2.3 49.7 %fused_product.1 = f32[16,8192]{1,0:T(8,128)S(1)} custom-call(s32[2,1,1,80]{3,2,1,0:T(1,128)S(1)} %copy-done.1, s32[1,1]{1,0:T(1,128)S(6)} %copy.6.count, s32[2,1,1,80]{3,2,1,0:T(1,128)S(1)} %copy-done.1, bf16[16,8192]{1,0:T(8,128)(2,1)S(1)} %bitcast.3, bf16[1,1,80,256,256]{4,3,2,1,0:T(8,128)(2,1)} %t_ref.1), custom_call_target="tpu_custom_call" | custom-call | tf_op jit(solution)/shard_map/fused_product/pallas_call | solution.py:297
  52.0 0.8 %copy.7 = f32[8192,16]{0,1:T(8,128)} copy(f32[8192,16]{0,1:T(8,128)S(1)} %bitcast.2) | data formatting | bytes 1048576
Async XLA Ops:
  0.7 1.0 %copy-start = (bf16[8192,16]{0,1:T(8,128)(2,1)S(1)}, bf16[8192,16]{0,1:T(8,128)(2,1)}, u32[]{:S(2)}) copy-start(bf16[8192,16]{0,1:T(8,128)(2,1)} %param.7) | copy-start | bytes 786436
  1.6 0.7 %copy-start.1 = (s32[2,1,1,80]{3,2,1,0:T(1,128)S(1)}, s32[2,1,1,80]{3,2,1,0:T(1,128)}, u32[]{:S(2)}) copy-start(s32[2,1,1,80]{3,2,1,0:T(1,128)} %coords_v.1) | copy-start | bytes 1924
